TPU v7x, 32 devices: a whole 2x2x4 slice. The times are simulated.
32 devices in a mesh: seq: 8 (over z, x), head: 4 (over y, core).
Axes of the slice: x: 2, y: 2, z: 4, core: 2. Of those that a mesh axis runs over, the one named last changes fastest.
Arguments:
- projections: bfloat16 [4096, 3, 4096], P('seq', None, 'head'), may hold values from -53 to 53
- output_gradient: bfloat16 [4096, 5120], P('seq', 'head'), may hold values from -0.75 to 0.75
- output_projection_weight: bfloat16 [5120, 4096], P(None, 'head'), may hold values from -0.625 to 0.625
- kept_token_indices: int32 [8, 192], P('seq'), may hold values from -1 to 511, as said below
- surviving_token_count: int32 [8], replicated, may hold values from 64 to 192, as said below
Outputs:
- projection_grad: bfloat16 [4096, 3, 4096], P('seq', None, 'head')
- weight_grad: float32 [5120, 4096], P('seq', 'head')
Inputs may be any that keep to these rules, and one draw needn't show every extreme that they name: `kept_token_indices`: row s holds, in its first surviving_token_count[s] entries, distinct indices 0 to 511 in ascending order; its other entries are -1. Every shard that keeps 192 tokens keeps its last token. `surviving_token_count`: some shard keeps exactly 192 tokens and some other keeps exactly 64.
All inputs are finite; a program needn't handle non-finite values.
Results may differ from a plain program's by a relative error of at most 0.0099.
Values may be sent and summed in bfloat16 or wider, within the bound.
No kernel may reach another device: no remote copies, remote signals or barrier semaphores. Data moves between devices by JAX's collectives and lax.ppermute only.
A program may use at most 128 MiB of HBM per device.

v0:
```python
import functools
import math

import jax
import jax.numpy as jnp
from jax import lax
from jax.experimental import pallas as pl
from jax.experimental.pallas import tpu as pltpu
from jax.sharding import PartitionSpec as P

DH = 128
QUERY_BLOCK = 256
WIDE_BLOCK = 512
VMEM_BYTES = 20 * 1024 * 1024
VMEM_MOST = 62 * 1024 * 1024
F32 = jnp.float32
BF16 = jnp.bfloat16


def params(limit=VMEM_BYTES):
    return pltpu.CompilerParams(vmem_limit_bytes=limit)


def dot(left, right):
    return jnp.dot(left, right, preferred_element_type=F32)


def dot_rows(left, right):
    return lax.dot_general(left, right, (((0,), (0,)), ((), ())), preferred_element_type=F32)


def dot_cols(left, right):
    return lax.dot_general(left, right, (((1,), (1,)), ((), ())), preferred_element_type=F32)


def token_selector(index_ref, tokens):
    slots = index_ref.shape[1]
    token = lax.broadcasted_iota(jnp.int32, (tokens, slots), 0)
    return jnp.where(token == index_ref[...], 1.0, 0.0).astype(BF16)


def pack_grad_kernel(index_ref, grad_ref, out_ref):
    selector = token_selector(index_ref, grad_ref.shape[0])
    out_ref[...] = dot_rows(selector, grad_ref[...]).astype(BF16)


def pack_grad(index, grad):
    slots = index.shape[1]
    return pl.pallas_call(
        pack_grad_kernel,
        out_shape=jax.ShapeDtypeStruct((slots, grad.shape[1]), BF16),
        compiler_params=params(),
    )(index, grad)


def pack_heads_kernel(index_ref, proj_ref, out_ref):
    selector = token_selector(index_ref, proj_ref.shape[1])
    for which in range(3):
        rows = dot_rows(selector, proj_ref[which]).astype(BF16)
        for head in range(out_ref.shape[0]):
            out_ref[head, :, which * DH : (which + 1) * DH] = rows[:, head * DH : (head + 1) * DH]


def pack_heads(index, proj):
    slots = index.shape[1]
    _, tokens, width = proj.shape
    heads = width // DH
    step = 2
    return pl.pallas_call(
        pack_heads_kernel,
        grid=(heads // step,),
        in_specs=[
            pl.BlockSpec((1, slots), lambda i: (0, 0)),
            pl.BlockSpec((3, tokens, step * DH), lambda i: (0, 0, i)),
        ],
        out_specs=pl.BlockSpec((step, slots, 3 * DH), lambda i: (i, 0, 0)),
        out_shape=jax.ShapeDtypeStruct((heads, slots, 3 * DH), BF16),
        compiler_params=params(),
    )(index, proj)


def unpack_heads_kernel(index_ref, rows_ref, out_ref):
    selector = token_selector(index_ref, out_ref.shape[1])
    for head in range(rows_ref.shape[0]):
        tokens = dot(selector, rows_ref[head]).astype(BF16)
        for which in range(3):
            out_ref[which, :, head * DH : (head + 1) * DH] = tokens[
                :, which * DH : (which + 1) * DH
            ]


def unpack_heads(index, rows, tokens):
    heads, slots, _ = rows.shape
    step = 2
    return pl.pallas_call(
        unpack_heads_kernel,
        grid=(heads // step,),
        in_specs=[
            pl.BlockSpec((1, slots), lambda i: (0, 0)),
            pl.BlockSpec((step, slots, 3 * DH), lambda i: (i, 0, 0)),
        ],
        out_specs=pl.BlockSpec((3, tokens, step * DH), lambda i: (0, 0, i)),
        out_shape=jax.ShapeDtypeStruct((3, tokens, heads * DH), BF16),
        compiler_params=params(),
    )(index, rows)


def grad_attn_kernel(rows_ref, weight_ref, out_ref):
    product = dot(rows_ref[...], weight_ref[...]).astype(BF16)
    for head in range(out_ref.shape[0]):
        out_ref[head] = product[:, head * DH : (head + 1) * DH]


def grad_attn_heads(rows, weight):
    slots, depth = rows.shape
    heads = weight.shape[1] // DH
    step = 2
    return pl.pallas_call(
        grad_attn_kernel,
        grid=(heads // step,),
        in_specs=[
            pl.BlockSpec((slots, depth), lambda i: (0, 0)),
            pl.BlockSpec((depth, step * DH), lambda i: (0, i)),
        ],
        out_specs=pl.BlockSpec((step, slots, DH), lambda i: (i, 0, 0)),
        out_shape=jax.ShapeDtypeStruct((heads, slots, DH), BF16),
        compiler_params=params(),
    )(rows, weight)


def weight_grad_kernel(rows_ref, attended_ref, out_ref):
    attended = jnp.concatenate([attended_ref[head] for head in range(attended_ref.shape[0])], axis=1)
    out_ref[...] = dot_rows(rows_ref[...], attended)


def weight_grad_heads(rows, attended):
    total, width = rows.shape
    heads = attended.shape[0]
    step = 2
    return pl.pallas_call(
        weight_grad_kernel,
        grid=(heads // step,),
        in_specs=[
            pl.BlockSpec((total, width), lambda i: (0, 0)),
            pl.BlockSpec((step, total, DH), lambda i: (i, 0, 0)),
        ],
        out_specs=pl.BlockSpec((width, step * DH), lambda i: (0, i)),
        out_shape=jax.ShapeDtypeStruct((width, heads * DH), F32),
        compiler_params=params(),
    )(rows, attended)


def attention_kernel(
    slots,
    part_rows,
    part_ref,
    live_ref,
    query_ref,
    grad_ref,
    key_ref,
    value_ref,
    attended_ref,
    query_grad_ref,
    key_grad_ref,
    value_grad_ref,
    key_total,
    value_total,
):
    scale = 1.0 / math.sqrt(DH)
    rows_total = query_ref.shape[0]
    keys_total = key_ref.shape[0]
    quarters = slots // part_rows
    key_flip = key_ref[...].T
    value_flip = value_ref[...].T
    for start in range(0, rows_total, QUERY_BLOCK):
        rows = slice(start, start + QUERY_BLOCK)
        last = start + QUERY_BLOCK - 1
        last_pos = last // part_rows * slots + (quarters - 1) * part_rows + last % part_rows
        first_pos = start // part_rows * slots + start % part_rows
        keys = min(-(-(last_pos + 1) // 128) * 128, keys_total)
        clear = first_pos // 128 * 128
        query = query_ref[rows]
        grad = grad_ref[rows]
        row = start + lax.broadcasted_iota(jnp.int32, (1, QUERY_BLOCK), 1)
        if quarters > 1:
            shard = row // part_rows
            row = shard * slots + part_ref[0] * part_rows + row - shard * part_rows
        scores = dot_cols(key_ref[:keys], query) * scale + live_ref[:keys, :1]
        key_pos = clear + lax.broadcasted_iota(jnp.int32, (keys - clear, 1), 0)
        edge = jnp.where(key_pos <= row, scores[clear:], -1e30)
        scores = jnp.concatenate([scores[:clear], edge], axis=0) if clear else edge
        peak = jnp.max(scores, axis=0, keepdims=True)
        weights = jnp.exp(scores - peak)
        probs = weights * (1.0 / jnp.sum(weights, axis=0, keepdims=True))
        probs_low = probs.astype(BF16)
        attended = dot(value_flip[:, :keys], probs_low)
        attended_ref[rows] = attended.T.astype(BF16)
        row_dot = jnp.sum(grad.T.astype(F32) * attended, axis=0, keepdims=True)
        grad_probs = dot_cols(value_ref[:keys], grad)
        grad_scores = (probs * (grad_probs - row_dot)).astype(BF16)
        query_grad = dot(key_flip[:, :keys], grad_scores) * scale
        query_grad_ref[rows] = query_grad.T.astype(BF16)
        key_part = dot(grad_scores, query)
        value_part = dot(probs_low, grad)
        prev = start - 1
        reached = 0
        if start:
            prev_pos = prev // part_rows * slots + (quarters - 1) * part_rows + prev % part_rows
            reached = min(-(-(prev_pos + 1) // 128) * 128, keys_total)
        if reached:
            key_total[:reached] += key_part[:reached]
            value_total[:reached] += value_part[:reached]
        if keys > reached:
            key_total[reached:keys] = key_part[reached:]
            value_total[reached:keys] = value_part[reached:]
    key_grad_ref[...] = (key_total[...] * scale).astype(key_grad_ref.dtype)
    value_grad_ref[...] = value_total[...].astype(value_grad_ref.dtype)


def attention(part, live, query, grad, key, value, slots, part_rows, key_type):
    rows, keys = query.shape[0], key.shape[0]
    vmem = pl.BlockSpec(memory_space=pltpu.VMEM)
    return pl.pallas_call(
        functools.partial(attention_kernel, slots, part_rows),
        in_specs=[pl.BlockSpec(memory_space=pltpu.SMEM)] + [vmem] * 5,
        out_specs=[vmem] * 4,
        out_shape=[
            jax.ShapeDtypeStruct((rows, DH), BF16),
            jax.ShapeDtypeStruct((rows, DH), BF16),
            jax.ShapeDtypeStruct((keys, DH), key_type),
            jax.ShapeDtypeStruct((keys, DH), key_type),
        ],
        scratch_shapes=[pltpu.VMEM((keys, DH), F32)] * 2,
        compiler_params=params(),
    )(part, live, query, grad, key, value)


def on_device_split_heads(
    projections,
    output_gradient,
    output_projection_weight,
    kept_token_indices,
    surviving_token_count,
):
    tok_dev = projections.shape[0]
    group_width = projections.shape[2]
    slots = kept_token_indices.shape[1]
    heads = group_width // DH
    seq_count = lax.axis_size("seq")
    head_count = lax.axis_size("head")
    quarters = seq_count // heads
    part_rows = slots // quarters
    part = (lax.axis_index("seq") % quarters).astype(jnp.int32).reshape(1)
    index = kept_token_indices
    keys = seq_count * slots

    grad_local = pack_grad(index, output_gradient)
    grad_rows = lax.all_gather(grad_local, "head", axis=1, tiled=True)
    packed = pack_heads(index, projections.transpose(1, 0, 2))

    position = jnp.arange(slots, dtype=jnp.int32)
    live = position[None, :] < surviving_token_count[:, None]
    live = jnp.where(live, 0.0, -1e30).astype(F32).reshape(keys, 1)
    live = jnp.broadcast_to(live, (keys, DH))

    def swap(blocks):
        return lax.all_to_all(blocks, "seq", split_axis=0, concat_axis=0, tiled=True)

    if quarters == 1:
        arrived = swap(packed).reshape(keys, 3 * DH)
        query, key, value = (arrived[:, n * DH : (n + 1) * DH] for n in range(3))
    else:
        query = swap(packed[:, :, :DH].reshape(seq_count, part_rows, DH))
        query = query.reshape(seq_count * part_rows, DH)
        sides = jnp.broadcast_to(packed[:, None, :, DH:], (heads, quarters, slots, 2 * DH))
        sides = swap(sides.reshape(seq_count, slots, 2 * DH)).reshape(keys, 2 * DH)
        key, value = sides[:, :DH], sides[:, DH:]

    grad_heads = grad_attn_heads(grad_rows, output_projection_weight)
    grad_in = swap(grad_heads.reshape(seq_count, part_rows, DH)).reshape(-1, DH)

    width = grad_rows.shape[1] // seq_count
    piece = slots // head_count
    mine = lax.dynamic_slice_in_dim(grad_rows, lax.axis_index("head") * piece, piece, 0)
    mine = swap(mine.reshape(piece, seq_count, width).transpose(1, 0, 2))
    all_rows = lax.all_gather(mine, "head", axis=1, tiled=True)

    key_type = BF16 if quarters == 1 else F32
    attended, query_grad, key_grad, value_grad = attention(
        part, live, query, grad_in, key, value, slots, part_rows, key_type
    )

    gathered = lax.all_gather(attended, "seq", axis=0).reshape(heads, keys, DH)
    all_rows = all_rows.reshape(seq_count, quarters, part_rows, width).transpose(1, 0, 2, 3)
    weight_grad = weight_grad_heads(all_rows.reshape(keys, width), gathered)

    if quarters == 1:
        back = jnp.concatenate([query_grad, key_grad, value_grad], axis=1)
        home = swap(back.reshape(seq_count, slots, 3 * DH))
    else:
        query_home = swap(query_grad.reshape(seq_count, part_rows, DH)).reshape(heads, slots, DH)
        back = jnp.concatenate([key_grad, value_grad], axis=1)
        key_home = swap(back.reshape(seq_count, slots, 2 * DH))
        key_home = jnp.sum(key_home.reshape(heads, quarters, slots, 2 * DH), axis=1)
        home = jnp.concatenate([query_home, key_home.astype(BF16)], axis=2)
    projection_grad = unpack_heads(index, home, tok_dev).transpose(1, 0, 2)
    return (projection_grad, weight_grad)


def pack_whole_kernel(index_ref, proj_ref, out_ref, loaded, packed, arrive, leave):
    parts = proj_ref.shape[0]
    copies = [
        pltpu.make_async_copy(proj_ref.at[which], loaded.at[which], arrive.at[which])
        for which in range(parts)
    ]
    for copy in copies:
        copy.start()
    token = lax.broadcasted_iota(jnp.int32, (loaded.shape[1], index_ref.shape[1]), 0)
    selector = jnp.where(token == index_ref[...], 1.0, 0.0).T.astype(BF16)
    away = []
    for which, copy in enumerate(copies):
        copy.wait()
        rows = dot(selector, loaded[which]).astype(BF16)
        for head in range(out_ref.shape[0]):
            packed[which, head] = rows[:, head * DH : (head + 1) * DH]
        away.append(
            pltpu.make_async_copy(
                packed.at[which],
                out_ref.at[:, :, which * DH : (which + 1) * DH],
                leave.at[which],
            )
        )
        away[-1].start()
    for copy in away:
        copy.wait()


def pack_whole(index, proj):
    slots = index.shape[1]
    parts, tokens, width = proj.shape
    heads = width // DH
    return pl.pallas_call(
        pack_whole_kernel,
        in_specs=[pl.BlockSpec(), pl.BlockSpec(memory_space=pltpu.HBM)],
        out_specs=pl.BlockSpec(memory_space=pltpu.HBM),
        out_shape=jax.ShapeDtypeStruct((heads, slots, parts * DH), BF16),
        scratch_shapes=[
            pltpu.VMEM(proj.shape, BF16),
            pltpu.VMEM((parts, heads, slots, DH), BF16),
            pltpu.SemaphoreType.DMA((parts,)),
            pltpu.SemaphoreType.DMA((parts,)),
        ],
        compiler_params=params(VMEM_MOST),
        cost_estimate=pl.CostEstimate(
            flops=2 * slots * tokens * parts * width,
            bytes_accessed=8 * tokens * width,
            transcendentals=0,
        ),
    )(index, proj)


def unpack_whole_kernel(index_ref, rows_ref, out_ref, tokens_ref, leave):
    selector = token_selector(index_ref, out_ref.shape[1])
    away = []
    for pair in range(rows_ref.shape[0] // 2):
        for side in range(2):
            tokens = dot(selector, rows_ref[2 * pair + side]).astype(BF16)
            for which in range(out_ref.shape[0]):
                tokens_ref[pair, which, :, side * DH : (side + 1) * DH] = tokens[
                    :, which * DH : (which + 1) * DH
                ]
        columns = pl.ds(pair * 2 * DH, 2 * DH)
        away.append(
            pltpu.make_async_copy(tokens_ref.at[pair], out_ref.at[:, :, columns], leave.at[pair])
        )
        away[-1].start()
    for copy in away:
        copy.wait()


def unpack_whole(index, rows, tokens):
    heads, slots, width = rows.shape
    parts = width // DH
    return pl.pallas_call(
        unpack_whole_kernel,
        in_specs=[VMEM_SPEC] * 2,
        out_specs=pl.BlockSpec(memory_space=pl.ANY),
        out_shape=jax.ShapeDtypeStruct((parts, tokens, heads * DH), BF16),
        scratch_shapes=[
            pltpu.VMEM((heads // 2, parts, tokens, 2 * DH), BF16),
            pltpu.SemaphoreType.DMA((heads // 2,)),
        ],
        compiler_params=params(),
    )(index, rows)


def exchange(block, axis, bit):
    return lax.ppermute(block, axis, [(i, i ^ bit) for i in range(lax.axis_size(axis))])


def gather_blocks(block, axis, bits, held=None):
    held = {0: block} if held is None else dict(held)
    reached = [0]
    for bit in bits:
        for step in list(reached):
            if step ^ bit not in held:
                held[step ^ bit] = exchange(held[step], axis, bit)
            reached.append(step ^ bit)
    return [held[step] for step in range(lax.axis_size(axis))]


SMEM_SPEC = pl.BlockSpec(memory_space=pltpu.SMEM)
VMEM_SPEC = pl.BlockSpec(memory_space=pltpu.VMEM)


def grad_swap_kernel(count, place_ref, *refs):
    row_refs, weight_ref, out_ref, total = refs[:count], refs[count], refs[count + 1], refs[count + 2]
    mine = place_ref[1]
    seq_count, height, _ = out_ref.shape
    slots, depth = row_refs[0].shape
    piece = slots // count
    chunks = (height - slots) // piece
    per_block = depth // (chunks * DH)
    for step in range(count):

        @pl.when(pl.program_id(0) == step)
        def _(step=step):
            part = dot(row_refs[step][...], weight_ref[...])
            total[...] = part if step == 0 else total[...] + part
            share = row_refs[step][pl.ds(pl.multiple_of(mine * piece, piece), piece), :]
            for chunk in range(per_block * chunks):
                partner = (mine ^ step) * per_block + chunk // chunks
                start = slots + chunk % chunks * piece
                out_ref[partner, start : start + piece, :] = share[:, chunk * DH : (chunk + 1) * DH]

    @pl.when(pl.program_id(0) == count - 1)
    def _():
        for head in range(seq_count):
            out_ref[head, :slots, :] = total[:, head * DH : (head + 1) * DH].astype(BF16)


def grad_swap(place, blocks, weight, seq_count):
    count = len(blocks)
    slots, depth = blocks[0].shape
    columns = weight.shape[1]
    height = slots + slots // count * (count * depth // seq_count // DH)
    return pl.pallas_call(
        functools.partial(grad_swap_kernel, count),
        grid_spec=pltpu.PrefetchScalarGridSpec(
            num_scalar_prefetch=1,
            grid=(count,),
            in_specs=[pl.BlockSpec((slots, depth), lambda i, place: (0, 0))] * count
            + [pl.BlockSpec((depth, columns), lambda i, place: (place[1] ^ i, 0))],
            out_specs=pl.BlockSpec((seq_count, height, DH), lambda i, place: (0, 0, 0)),
            scratch_shapes=[pltpu.VMEM((slots, columns), F32)],
        ),
        out_shape=jax.ShapeDtypeStruct((seq_count, height, DH), BF16),
        compiler_params=params(),
        cost_estimate=pl.CostEstimate(
            flops=2 * slots * count * depth * columns,
            bytes_accessed=2 * count * depth * columns,
            transcendentals=0,
        ),
    )(place, *blocks, weight)


def flip_rows_kernel(place_ref, *refs):
    piece_refs, out_ref, rows = refs[:-2], refs[-2], refs[-1]
    count = len(piece_refs)
    chunks = rows.shape[1] // DH
    shards, height, _ = piece_refs[0].shape
    piece = height // chunks
    for part in range(count):
        for shard in range(shards):
            start = shard * piece * count + (place_ref[1] ^ part) * piece
            here = pl.ds(pl.multiple_of(start, piece), piece)
            for chunk in range(chunks):
                rows[here, chunk * DH : (chunk + 1) * DH] = piece_refs[part][
                    shard, chunk * piece : (chunk + 1) * piece, :
                ]
    out_ref[...] = rows[...].T


def flip_rows(place, pieces, slots):
    shards, height, _ = pieces[0].shape
    width = height // (slots // len(pieces)) * DH
    keys = shards * slots
    return pl.pallas_call(
        flip_rows_kernel,
        in_specs=[SMEM_SPEC] + [pl.BlockSpec()] * len(pieces),
        out_specs=VMEM_SPEC,
        out_shape=jax.ShapeDtypeStruct((width, keys), BF16),
        scratch_shapes=[pltpu.VMEM((keys, width), BF16)],
        compiler_params=params(),
        cost_estimate=pl.CostEstimate(flops=0, bytes_accessed=4 * keys * width, transcendentals=0),
    )(place, *pieces)


def weight_part_kernel(first, count, place_ref, flip_ref, *refs):
    out_ref, product_ref, leave = refs[-3:]
    away = []
    for step in range(0, count, 2):
        both = jnp.concatenate([ref[...] for ref in refs[step : step + 2]], axis=1)
        product = dot(flip_ref[...], both)
        head = place_ref[0] ^ (first + step)
        for side in range(2):
            column = pl.multiple_of((head ^ side) % 2 * DH, DH)
            product_ref[step // 2, :, pl.ds(column, DH)] = product[:, side * DH : (side + 1) * DH]
        columns = pl.ds(pl.multiple_of(head // 2 * (2 * DH), 2 * DH), 2 * DH)
        away.append(
            pltpu.make_async_copy(
                product_ref.at[step // 2], out_ref.at[:, columns], leave.at[step // 2]
            )
        )
        away[-1].start()
    for copy in away:
        copy.wait()


def weight_part(place, flip, attended, first, heads, weight, before=None):
    count = len(attended)
    width, keys = flip.shape
    more = [] if before is None else [before]
    return pl.pallas_call(
        functools.partial(weight_part_kernel, first, count),
        in_specs=[SMEM_SPEC]
        + [VMEM_SPEC] * (1 + count)
        + [pl.BlockSpec(memory_space=pl.ANY)] * len(more),
        out_specs=pl.BlockSpec(memory_space=pl.ANY),
        out_shape=jax.ShapeDtypeStruct((width, heads * DH), F32),
        scratch_shapes=[
            pltpu.VMEM((count // 2, width, 2 * DH), F32),
            pltpu.SemaphoreType.DMA((count // 2,)),
        ],
        input_output_aliases={2 + count: 0} if more else {},
        compiler_params=params(),
        cost_estimate=pl.CostEstimate(
            flops=weight * 2 * keys * width * count * DH,
            bytes_accessed=8 * keys * DH * count,
            transcendentals=0,
        ),
    )(place, flip, *attended, *more)


def mark_live(count_ref, live_ref, slots):
    for shard in range(live_ref.shape[0] // slots):
        inside = lax.broadcasted_iota(jnp.int32, (slots, live_ref.shape[1]), 0)
        live_ref[shard * slots : (shard + 1) * slots] = jnp.where(
            inside < count_ref[shard], 0.0, -1e30
        )


def masked_scores(start, keys, key_ref, query, live_ref):
    scores = dot_cols(key_ref[:keys], query) * (1.0 / math.sqrt(DH)) + live_ref[:keys, :1]
    row = start + lax.broadcasted_iota(jnp.int32, (1, WIDE_BLOCK), 1)
    key_pos = start + lax.broadcasted_iota(jnp.int32, (WIDE_BLOCK, 1), 0)
    edge = jnp.where(key_pos <= row, scores[start:], -1e30)
    return jnp.concatenate([scores[:start], edge], axis=0) if start else edge


def split_blocks(block_ref, *refs):
    shards, slots, _ = block_ref.shape
    for shard in range(shards):
        for which, ref in enumerate(refs):
            ref[shard * slots : (shard + 1) * slots] = block_ref[
                shard, :, which * DH : (which + 1) * DH
            ]


def forward_kernel(
    count_ref, block_ref, attended_ref, stat_ref, live_ref, query_ref, key_ref, value_ref
):
    mark_live(count_ref, live_ref, block_ref.shape[1])
    split_blocks(block_ref, query_ref, key_ref, value_ref)
    value_flip = value_ref[...].T
    for start in range(0, query_ref.shape[0], WIDE_BLOCK):
        rows = slice(start, start + WIDE_BLOCK)
        keys = start + WIDE_BLOCK
        scores = masked_scores(start, keys, key_ref, query_ref[rows], live_ref)
        peak = jnp.max(scores, axis=0, keepdims=True)
        weights = jnp.exp(scores - peak)
        inverse = 1.0 / jnp.sum(weights, axis=0, keepdims=True)
        attended = dot(value_flip[:, :keys], (weights * inverse).astype(BF16))
        attended_ref[rows] = attended.T.astype(BF16)
        stat_ref[0:1, rows] = peak
        stat_ref[1:2, rows] = inverse


def attention_cost(keys, dots):
    return pl.CostEstimate(
        flops=dots * keys * keys * DH, bytes_accessed=16 * keys * DH, transcendentals=keys * keys // 2
    )


def forward(counts, blocks):
    keys = blocks.shape[0] * blocks.shape[1]
    return pl.pallas_call(
        forward_kernel,
        out_shape=[
            jax.ShapeDtypeStruct((keys, DH), BF16),
            jax.ShapeDtypeStruct((8, keys), F32),
        ],
        in_specs=[SMEM_SPEC, pl.BlockSpec()],
        scratch_shapes=[pltpu.VMEM((keys, DH), F32)] + [pltpu.VMEM((keys, DH), BF16)] * 3,
        compiler_params=params(32 * 1024 * 1024),
        cost_estimate=attention_cost(keys, 2),
    )(counts, blocks)


def backward_kernel(
    count_ref,
    block_ref,
    attended_ref,
    stat_ref,
    grads_ref,
    out_ref,
    live_ref,
    query_ref,
    key_ref,
    value_ref,
    grad_ref,
    query_total,
    key_total,
    value_total,
):
    seq_count, slots, _ = out_ref.shape
    scale = 1.0 / math.sqrt(DH)
    mark_live(count_ref, live_ref, slots)
    split_blocks(block_ref, query_ref, key_ref, value_ref)
    for shard in range(seq_count):
        grad_ref[shard * slots : (shard + 1) * slots] = grads_ref[shard, :slots]
    key_flip = key_ref[...].T
    for start in range(0, query_ref.shape[0], WIDE_BLOCK):
        rows = slice(start, start + WIDE_BLOCK)
        keys = start + WIDE_BLOCK
        query = query_ref[rows]
        grad = grad_ref[rows]
        scores = masked_scores(start, keys, key_ref, query, live_ref)
        probs = jnp.exp(scores - stat_ref[0:1, rows]) * stat_ref[1:2, rows]
        probs_low = probs.astype(BF16)
        product = grad.astype(F32) * attended_ref[rows].astype(F32)
        row_dot = jnp.sum(product.T, axis=0, keepdims=True)
        grad_probs = dot_cols(value_ref[:keys], grad)
        grad_scores = (probs * (grad_probs - row_dot)).astype(BF16)
        query_total[rows] = (dot(key_flip[:, :keys], grad_scores) * scale).T.astype(BF16)
        key_part = dot(grad_scores, query)
        value_part = dot(probs_low, grad)
        if start:
            key_total[:start] += key_part[:start]
            value_total[:start] += value_part[:start]
        key_total[rows] = key_part[start:]
        value_total[rows] = value_part[start:]
    for shard in range(seq_count):
        here = slice(shard * slots, (shard + 1) * slots)
        out_ref[shard, :, :DH] = query_total[here]
        out_ref[shard, :, DH : 2 * DH] = (key_total[here] * scale).astype(BF16)
        out_ref[shard, :, 2 * DH :] = value_total[here].astype(BF16)


def backward(counts, blocks, attended, stats, grads):
    keys = attended.shape[0]
    return pl.pallas_call(
        backward_kernel,
        in_specs=[SMEM_SPEC] + [pl.BlockSpec()] * 4,
        out_shape=jax.ShapeDtypeStruct(blocks.shape, BF16),
        scratch_shapes=[pltpu.VMEM((keys, DH), F32)]
        + [pltpu.VMEM((keys, DH), BF16)] * 5
        + [pltpu.VMEM((keys, DH), F32)] * 2,
        compiler_params=params(VMEM_MOST),
        cost_estimate=attention_cost(keys, 5),
    )(counts, blocks, attended, stats, grads)


def on_device_whole_heads(
    projections,
    output_gradient,
    output_projection_weight,
    kept_token_indices,
    surviving_token_count,
):
    tok_dev = projections.shape[0]
    slots = kept_token_indices.shape[1]
    seq_count = lax.axis_size("seq")
    head_count = lax.axis_size("head")
    index = kept_token_indices
    place = jnp.stack([lax.axis_index("seq"), lax.axis_index("head")]).astype(jnp.int32)
    seq_bits = [1 << bit for bit in reversed(range(seq_count.bit_length() - 1))]
    head_bits = [1 << bit for bit in reversed(range(head_count.bit_length() - 1))]

    def swap(blocks):
        return lax.all_to_all(blocks, "seq", split_axis=0, concat_axis=0, tiled=True)

    packed = pack_whole(index, projections.transpose(1, 0, 2))
    packed, grad_index = lax.optimization_barrier((packed, index))
    arrived = swap(packed)
    grad_blocks = gather_blocks(pack_grad(grad_index, output_gradient), "head", head_bits)
    grads = swap(grad_swap(place, grad_blocks, output_projection_weight, seq_count))
    attended, stats = forward(surviving_token_count, arrived)

    near, last = seq_bits[-2], seq_bits[-1]
    held = {bit: exchange(attended, "seq", bit) for bit in seq_bits}
    held[near ^ last] = exchange(held[near], "seq", last)
    back = backward(surviving_token_count, arrived, attended, stats, grads)
    back, held = lax.optimization_barrier((back, held))
    gathered = gather_blocks(attended, "seq", seq_bits, {0: attended, **held})
    home = swap(back)
    pieces = gather_blocks(grads[:, slots:], "head", head_bits)
    flip = flip_rows(place, pieces, slots)
    late = seq_count - 2
    weight_grad = weight_part(place, flip, gathered[:late], 0, seq_count, 1)
    projection_grad = unpack_whole(index, home, tok_dev)
    weight_grad = weight_part(place, flip, gathered[late:], late, seq_count, 28, weight_grad)
    projection_grad = projection_grad.transpose(1, 0, 2)
    return (projection_grad, weight_grad)


def on_device(projections, output_gradient, weight, index, counts):
    heads = projections.shape[2] // DH
    seq_count, head_count = lax.axis_size("seq"), lax.axis_size("head")
    width = output_gradient.shape[1] * head_count // seq_count
    whole = seq_count == heads and seq_count % 2 == 0 and width % DH == 0
    powers = seq_count & (seq_count - 1) == 0 and head_count & (head_count - 1) == 0
    body = on_device_whole_heads if whole and powers else on_device_split_heads
    return body(projections, output_gradient, weight, index, counts)


def solution(mesh):
    return jax.shard_map(
        on_device,
        mesh=mesh,
        in_specs=(P("seq", None, "head"), P("seq", "head"), P(None, "head"), P("seq", None), P()),
        out_specs=(P("seq", None, "head"), P("seq", "head")),
        check_vma=False,
    )
```

profile of v0, /device:TPU:0, one launch (start us, length us, event | category | flops | bytes accessed | tf_op | source)
XLA Modules:
  0.0 125.2 jit_solution(16387160179572768559)
XLA Ops:
  0.6 3.9 %shard_map.68 = bf16[8,192,384]{2,1,0:T(8,128)(2,1)} custom-call(s32[1,192]{1,0:T(1,128)} %index_ref.4, bf16[3,512,1024]{2,1,0:T(8,128)(2,1)} %bitcast.4), custom_call_target="tpu_custom_call" | custom-call | flops 603979776 | bytes 4194304 | tf_op jit(solution)/shard_map/pallas_call | solution.py:342
  4.5 7.4 %all-to-all-start = ((bf16[8,192,384]{2,1,0:T(8,128)(2,1)}), bf16[8,192,384]{2,1,0:T(8,128)(2,1)S(1)}, u32[]{:S(2)}, u32[]{:S(2)}) async-start(bf16[8,192,384]{2,1,0:T(8,128)(2,1)} %shard_map.68), calls=%async_computation | async-start | bytes 2359296 | tf_op jit(solution)/shard_map/all_to_all | solution.py:691
  12.4 1.6 %collective-permute-start.1 = (bf16[192,1280]{1,0:T(8,128)(2,1)S(1)}, bf16[192,1280]{1,0:T(8,128)(2,1)S(1)}, u32[]{:S(2)}, u32[]{:S(2)}) collective-permute-start(bf16[192,1280]{1,0:T(8,128)(2,1)S(1)} %shard_map.70.refs_0_), channel_id=1, source_target_pairs={{0,2},{1,3},{2,0},{3,1},{4,6},{5,7},{6,4},{7,5},{8,10},{9,11},{10,... | collective-permute-start | bytes 1474568 | tf_op jit(solution)/shard_map/ppermute | solution.py:398
  14.0 11.2 %collective-permute-done.1.refs_2_ = bf16[192,1280]{1,0:T(8,128)(2,1)S(1)} collective-permute-done((bf16[192,1280]{1,0:T(8,128)(2,1)S(1)}, bf16[192,1280]{1,0:T(8,128)(2,1)S(1)}, u32[]{:S(2)}, u32[]{:S(2)}) %collective-permute-start.1) | collective-permute-done | bytes 491552 | tf_op jit(solution)/shard_map/ppermute | solution.py:398
  25.2 1.8 %collective-permute-done.2.refs_3_ = bf16[192,1280]{1,0:T(8,128)(2,1)S(1)} collective-permute-done((bf16[192,1280]{1,0:T(8,128)(2,1)S(1)}, bf16[192,1280]{1,0:T(8,128)(2,1)S(1)}, u32[]{:S(2)}, u32[]{:S(2)}) %collective-permute-start.2) | collective-permute-done | bytes 491552 | tf_op jit(solution)/shard_map/ppermute | solution.py:398
  27.0 4.0 %copy-done = bf16[5120,1024]{1,0:T(8,128)(2,1)S(1)} copy-done((bf16[5120,1024]{1,0:T(8,128)(2,1)S(1)}, bf16[5120,1024]{1,0:T(8,128)(2,1)}, u32[]{:S(2)}) %copy-start) | copy-done | bytes 10485784
  31.0 4.4 %shard_map.71 = bf16[8,432,128]{2,1,0:T(8,128)(2,1)} custom-call(s32[2]{0:T(128)S(1)} %pad_add_fusion.place_ref, bf16[192,1280]{1,0:T(8,128)(2,1)S(1)} %shard_map.70.refs_0_, bf16[192,1280]{1,0:T(8,128)(2,1)S(1)} %collective-permute-done.refs_1_, bf16[192,1280]{1,0:T(8,128)(2,1)S(1)} %collective-permute-done.1.refs_2_, ...), custom_call_target="tpu_custom_call" | custom-call | flops 2013265920 | bytes 10485760 | tf_op jit(solution)/shard_map/pallas_call | solution.py:447
  35.4 5.1 %all-to-all-done.block_ref = bf16[8,192,384]{2,1,0:T(8,128)(2,1)S(1)} async-done(((bf16[8,192,384]{2,1,0:T(8,128)(2,1)}), bf16[8,192,384]{2,1,0:T(8,128)(2,1)S(1)}, u32[]{:S(2)}, u32[]{:S(2)}) %all-to-all-start) | async-done | bytes 1179680 | tf_op jit(solution)/shard_map/all_to_all | solution.py:691
  40.5 4.2 %all-to-all-start.1 = ((bf16[8,432,128]{2,1,0:T(8,128)(2,1)}), bf16[8,432,128]{2,1,0:T(8,128)(2,1)}, u32[]{:S(2)}, u32[]{:S(2)}) async-start(bf16[8,432,128]{2,1,0:T(8,128)(2,1)} %shard_map.71), calls=%async_computation.1 | async-start | bytes 1769472 | tf_op jit(solution)/shard_map/all_to_all | solution.py:691
  44.7 4.3 %shard_map.69 = (bf16[1536,128]{1,0:T(8,128)(2,1)}, f32[8,1536]{1,0:T(8,128)S(1)}) custom-call(s32[8]{0:T(128)S(1)} %copy-done.4, bf16[8,192,384]{2,1,0:T(8,128)(2,1)S(1)} %all-to-all-done.block_ref), custom_call_target="tpu_custom_call" | custom-call | flops 603979776 | bytes 3145728 | tf_op jit(solution)/shard_map/pallas_call | solution.py:597
  49.7 1.9 %collective-permute-start.4 = (bf16[1536,128]{1,0:T(8,128)(2,1)}, bf16[1536,128]{1,0:T(8,128)(2,1)S(1)}, u32[]{:S(2)}, u32[]{:S(2)}) collective-permute-start(bf16[1536,128]{1,0:T(8,128)(2,1)} %get-tuple-element.12.attended_ref.refs_0_), channel_id=1, source_target_pairs={{0,8},{4,12},{8,0},{12,4},{16,24},{20,28},{24,16},{28,20},{1,9},{5... | collective-permute-start | bytes 1179656 | tf_op jit(solution)/shard_map/ppermute | solution.py:398
  51.5 2.4 %collective-permute-start.6 = (bf16[1536,128]{1,0:T(8,128)(2,1)}, bf16[1536,128]{1,0:T(8,128)(2,1)S(1)}, u32[]{:S(2)}, u32[]{:S(2)}) collective-permute-start(bf16[1536,128]{1,0:T(8,128)(2,1)} %get-tuple-element.12.attended_ref.refs_0_), channel_id=1, source_target_pairs={{0,16},{4,20},{8,24},{12,28},{16,0},{20,4},{24,8},{28,12},{1,17},{... | collective-permute-start | bytes 1179656 | tf_op jit(solution)/shard_map/ppermute | solution.py:398
  55.4 18.4 %collective-permute-done.4.refs_2_ = bf16[1536,128]{1,0:T(8,128)(2,1)S(1)} collective-permute-done((bf16[1536,128]{1,0:T(8,128)(2,1)}, bf16[1536,128]{1,0:T(8,128)(2,1)S(1)}, u32[]{:S(2)}, u32[]{:S(2)}) %collective-permute-start.4) | collective-permute-done | bytes 393248 | tf_op jit(solution)/shard_map/ppermute | solution.py:398
  73.9 1.7 %collective-permute-start.5 = (bf16[1536,128]{1,0:T(8,128)(2,1)S(1)}, bf16[1536,128]{1,0:T(8,128)(2,1)}, u32[]{:S(2)}, u32[]{:S(2)}) collective-permute-start(bf16[1536,128]{1,0:T(8,128)(2,1)S(1)} %collective-permute-done.4.refs_2_), channel_id=1, source_target_pairs={{0,4},{4,0},{8,12},{12,8},{16,20},{20,16},{24,28},{28,24},{1,5},{5... | collective-permute-start | bytes 1179656 | tf_op jit(solution)/shard_map/ppermute | solution.py:398
  76.7 1.6 %collective-permute-start.8 = (bf16[8,240,128]{2,1,0:T(8,128)(2,1)S(1)}, bf16[8,240,128]{2,1,0:T(8,128)(2,1)S(1)}, u32[]{:S(2)}, u32[]{:S(2)}) collective-permute-start(bf16[8,240,128]{2,1,0:T(8,128)(2,1)S(1)} %slice.4.refs_0_), channel_id=1, source_target_pairs={{0,2},{1,3},{2,0},{3,1},{4,6},{5,7},{6,4},{7,5},{8,10},{9,11},{10,... | collective-permute-start | bytes 1474568 | tf_op jit(solution)/shard_map/ppermute | solution.py:398
  78.2 7.5 %shard_map.72 = bf16[8,192,384]{2,1,0:T(8,128)(2,1)} custom-call(s32[8]{0:T(128)} %count_ref.3, bf16[8,192,384]{2,1,0:T(8,128)(2,1)} %copy-done.2, bf16[1536,128]{1,0:T(8,128)(2,1)} %get-tuple-element.12.attended_ref.refs_0_, f32[8,1536]{1,0:T(8,128)} %copy-done.5, bf16[8,432,128]{2,1,0:T(8,128)(2,1)} %all-to-all-done.1.grads_ref), custom_call_target="tpu_custom_call" | custom-call | flops 1509949440 | bytes 3145728 | tf_op jit(solution)/shard_map/pallas_call | solution.py:662
  85.9 3.8 %all-to-all-start.2 = ((bf16[8,192,384]{2,1,0:T(8,128)(2,1)}), bf16[8,192,384]{2,1,0:T(8,128)(2,1)S(1)}, u32[]{:S(2)}, u32[]{:S(2)}) async-start(bf16[8,192,384]{2,1,0:T(8,128)(2,1)} %shard_map.72), calls=%async_computation.2 | async-start | bytes 2359296 | tf_op jit(solution)/shard_map/all_to_all | solution.py:691
  90.2 1.7 %collective-permute-start.12 = (bf16[1536,128]{1,0:T(8,128)(2,1)S(1)}, bf16[1536,128]{1,0:T(8,128)(2,1)S(1)}, u32[]{:S(2)}, u32[]{:S(2)}) collective-permute-start(bf16[1536,128]{1,0:T(8,128)(2,1)S(1)} %collective-permute-done.6.refs_4_), channel_id=1, source_target_pairs={{0,4},{4,0},{8,12},{12,8},{16,20},{20,16},{24,28},{28,24},{1,5},{5... | collective-permute-start | bytes 1179656 | tf_op jit(solution)/shard_map/ppermute | solution.py:398
  91.9 13.5 %collective-permute-done.10.refs_0_ = bf16[1536,128]{1,0:T(8,128)(2,1)} collective-permute-done((bf16[1536,128]{1,0:T(8,128)(2,1)S(1)}, bf16[1536,128]{1,0:T(8,128)(2,1)}, u32[]{:S(2)}, u32[]{:S(2)}) %collective-permute-start.10) | collective-permute-done | bytes 393248 | tf_op jit(solution)/shard_map/ppermute | solution.py:398
  106.9 6.6 %collective-permute-done.12.refs_5_ = bf16[1536,128]{1,0:T(8,128)(2,1)S(1)} collective-permute-done((bf16[1536,128]{1,0:T(8,128)(2,1)S(1)}, bf16[1536,128]{1,0:T(8,128)(2,1)S(1)}, u32[]{:S(2)}, u32[]{:S(2)}) %collective-permute-start.12) | collective-permute-done | bytes 393248 | tf_op jit(solution)/shard_map/ppermute | solution.py:398
  113.5 4.0 %shard_map.75.refs_2_ = f32[640,1024]{1,0:T(8,128)} custom-call(s32[2]{0:T(128)S(1)} %pad_add_fusion.place_ref, bf16[640,1536]{1,0:T(8,128)(2,1)S(1)} %shard_map.74.flip_ref, bf16[1536,128]{1,0:T(8,128)(2,1)} %get-tuple-element.12.attended_ref.refs_0_, bf16[1536,128]{1,0:T(8,128)(2,1)} %collective-permute-done.3.refs_1_, ...), custom_call_target="tpu_custom_call" | custom-call | flops 1509949440 | bytes 9437184 | tf_op jit(solution)/shard_map/pallas_call | solution.py:524
  117.6 2.8 %collective-permute-done.11.refs_1_ = bf16[1536,128]{1,0:T(8,128)(2,1)S(1)} collective-permute-done((bf16[1536,128]{1,0:T(8,128)(2,1)}, bf16[1536,128]{1,0:T(8,128)(2,1)S(1)}, u32[]{:S(2)}, u32[]{:S(2)}) %collective-permute-start.11) | collective-permute-done | bytes 393248 | tf_op jit(solution)/shard_map/ppermute | solution.py:398
  120.4 2.5 %shard_map.76 = f32[640,1024]{1,0:T(8,128)} custom-call(s32[2]{0:T(128)S(1)} %pad_add_fusion.place_ref, bf16[640,1536]{1,0:T(8,128)(2,1)S(1)} %shard_map.74.flip_ref, bf16[1536,128]{1,0:T(8,128)(2,1)} %collective-permute-done.10.refs_0_, bf16[1536,128]{1,0:T(8,128)(2,1)S(1)} %collective-permute-done.11.refs_1_, ...), custom_call_target="tpu_custom_call", output_to_operand_aliasing={{}: (4, {})} | custom-call | flops 14092861440 | bytes 3145728 | tf_op jit(solution)/shard_map/pallas_call | solution.py:524
  122.9 2.2 %shard_map.73 = bf16[3,512,1024]{2,1,0:T(8,128)(2,1)} custom-call(s32[1,192]{1,0:T(1,128)S(1)} %copy-done.3, bf16[8,192,384]{2,1,0:T(8,128)(2,1)S(1)} %all-to-all-done.2.rows_ref), custom_call_target="tpu_custom_call" | custom-call | tf_op jit(solution)/shard_map/pallas_call | solution.py:384
  (31 shorter events, 5.8 us)
Async XLA Ops:
  4.5 7.4 %copy-start.1 = (bf16[512,1280]{1,0:T(8,128)(2,1)S(1)}, bf16[512,1280]{1,0:T(8,128)(2,1)}, u32[]{:S(2)}) copy-start(bf16[512,1280]{1,0:T(8,128)(2,1)} %grad_ref.1) | copy-start | bytes 3932164
  4.5 7.4 %copy-start.3 = (s32[1,192]{1,0:T(1,128)S(1)}, s32[1,192]{1,0:T(1,128)}, u32[]{:S(2)}) copy-start(s32[1,192]{1,0:T(1,128)} %index_ref.4) | copy-start | bytes 2308
  4.5 36.0 %all-to-all-start = ((bf16[8,192,384]{2,1,0:T(8,128)(2,1)}), bf16[8,192,384]{2,1,0:T(8,128)(2,1)S(1)}, u32[]{:S(2)}, u32[]{:S(2)}) async-start(bf16[8,192,384]{2,1,0:T(8,128)(2,1)} %shard_map.68), calls=%async_computation | async-start | bytes 2359296 | tf_op jit(solution)/shard_map/all_to_all | solution.py:691
  12.4 12.7 %collective-permute-start.1 = (bf16[192,1280]{1,0:T(8,128)(2,1)S(1)}, bf16[192,1280]{1,0:T(8,128)(2,1)S(1)}, u32[]{:S(2)}, u32[]{:S(2)}) collective-permute-start(bf16[192,1280]{1,0:T(8,128)(2,1)S(1)} %shard_map.70.refs_0_), channel_id=1, source_target_pairs={{0,2},{1,3},{2,0},{3,1},{4,6},{5,7},{6,4},{7,5},{8,10},{9,11},{10,... | collective-permute-start | bytes 1474568 | tf_op jit(solution)/shard_map/ppermute | solution.py:398
  14.0 11.2 %collective-permute-start = (bf16[192,1280]{1,0:T(8,128)(2,1)S(1)}, bf16[192,1280]{1,0:T(8,128)(2,1)S(1)}, u32[]{:S(2)}, u32[]{:S(2)}) collective-permute-start(bf16[192,1280]{1,0:T(8,128)(2,1)S(1)} %shard_map.70.refs_0_), channel_id=1, source_target_pairs={{0,1},{1,0},{2,3},{3,2},{4,5},{5,4},{6,7},{7,6},{8,9},{9,8},{10,11... | collective-permute-start | bytes 1474568 | tf_op jit(solution)/shard_map/ppermute | solution.py:398
  25.1 1.9 %collective-permute-start.2 = (bf16[192,1280]{1,0:T(8,128)(2,1)S(1)}, bf16[192,1280]{1,0:T(8,128)(2,1)S(1)}, u32[]{:S(2)}, u32[]{:S(2)}) collective-permute-start(bf16[192,1280]{1,0:T(8,128)(2,1)S(1)} %collective-permute-done.1.refs_2_), channel_id=1, source_target_pairs={{0,1},{1,0},{2,3},{3,2},{4,5},{5,4},{6,7},{7,6},{8,9},{9,8},{10,11... | collective-permute-start | bytes 1474568 | tf_op jit(solution)/shard_map/ppermute | solution.py:398
  25.1 19.6 %copy-start.4 = (s32[8]{0:T(128)S(1)}, s32[8]{0:T(128)}, u32[]{:S(2)}) copy-start(s32[8]{0:T(128)} %count_ref.3) | copy-start | bytes 100
  27.0 4.0 %copy-start = (bf16[5120,1024]{1,0:T(8,128)(2,1)S(1)}, bf16[5120,1024]{1,0:T(8,128)(2,1)}, u32[]{:S(2)}) copy-start(bf16[5120,1024]{1,0:T(8,128)(2,1)} %refs_4_.1) | copy-start | bytes 31457284
  40.5 8.6 %copy-start.2 = (bf16[8,192,384]{2,1,0:T(8,128)(2,1)}, bf16[8,192,384]{2,1,0:T(8,128)(2,1)S(1)}, u32[]{:S(2)}) copy-start(bf16[8,192,384]{2,1,0:T(8,128)(2,1)S(1)} %all-to-all-done.block_ref) | copy-start | bytes 3538948
  40.5 35.1 %all-to-all-start.1 = ((bf16[8,432,128]{2,1,0:T(8,128)(2,1)}), bf16[8,432,128]{2,1,0:T(8,128)(2,1)}, u32[]{:S(2)}, u32[]{:S(2)}) async-start(bf16[8,432,128]{2,1,0:T(8,128)(2,1)} %shard_map.71), calls=%async_computation.1 | async-start | bytes 1769472 | tf_op jit(solution)/shard_map/all_to_all | solution.py:691
  49.0 0.6 copy-start.5
  49.7 24.2 %collective-permute-start.4 = (bf16[1536,128]{1,0:T(8,128)(2,1)}, bf16[1536,128]{1,0:T(8,128)(2,1)S(1)}, u32[]{:S(2)}, u32[]{:S(2)}) collective-permute-start(bf16[1536,128]{1,0:T(8,128)(2,1)} %get-tuple-element.12.attended_ref.refs_0_), channel_id=1, source_target_pairs={{0,8},{4,12},{8,0},{12,4},{16,24},{20,28},{24,16},{28,20},{1,9},{5... | collective-permute-start | bytes 1179656 | tf_op jit(solution)/shard_map/ppermute | solution.py:398
  51.5 34.2 %collective-permute-start.6 = (bf16[1536,128]{1,0:T(8,128)(2,1)}, bf16[1536,128]{1,0:T(8,128)(2,1)S(1)}, u32[]{:S(2)}, u32[]{:S(2)}) collective-permute-start(bf16[1536,128]{1,0:T(8,128)(2,1)} %get-tuple-element.12.attended_ref.refs_0_), channel_id=1, source_target_pairs={{0,16},{4,20},{8,24},{12,28},{16,0},{20,4},{24,8},{28,12},{1,17},{... | collective-permute-start | bytes 1179656 | tf_op jit(solution)/shard_map/ppermute | solution.py:398
  53.9 31.8 %collective-permute-start.3 = (bf16[1536,128]{1,0:T(8,128)(2,1)}, bf16[1536,128]{1,0:T(8,128)(2,1)}, u32[]{:S(2)}, u32[]{:S(2)}) collective-permute-start(bf16[1536,128]{1,0:T(8,128)(2,1)} %get-tuple-element.12.attended_ref.refs_0_), channel_id=1, source_target_pairs={{0,4},{4,0},{8,12},{12,8},{16,20},{20,16},{24,28},{28,24},{1,5},{5... | collective-permute-start | bytes 1179656 | tf_op jit(solution)/shard_map/ppermute | solution.py:398
  73.9 11.9 %collective-permute-start.5 = (bf16[1536,128]{1,0:T(8,128)(2,1)S(1)}, bf16[1536,128]{1,0:T(8,128)(2,1)}, u32[]{:S(2)}, u32[]{:S(2)}) collective-permute-start(bf16[1536,128]{1,0:T(8,128)(2,1)S(1)} %collective-permute-done.4.refs_2_), channel_id=1, source_target_pairs={{0,4},{4,0},{8,12},{12,8},{16,20},{20,16},{24,28},{28,24},{1,5},{5... | collective-permute-start | bytes 1179656 | tf_op jit(solution)/shard_map/ppermute | solution.py:398
  76.7 13.1 %collective-permute-start.8 = (bf16[8,240,128]{2,1,0:T(8,128)(2,1)S(1)}, bf16[8,240,128]{2,1,0:T(8,128)(2,1)S(1)}, u32[]{:S(2)}, u32[]{:S(2)}) collective-permute-start(bf16[8,240,128]{2,1,0:T(8,128)(2,1)S(1)} %slice.4.refs_0_), channel_id=1, source_target_pairs={{0,2},{1,3},{2,0},{3,1},{4,6},{5,7},{6,4},{7,5},{8,10},{9,11},{10,... | collective-permute-start | bytes 1474568 | tf_op jit(solution)/shard_map/ppermute | solution.py:398
  85.8 19.6 %collective-permute-start.10 = (bf16[1536,128]{1,0:T(8,128)(2,1)S(1)}, bf16[1536,128]{1,0:T(8,128)(2,1)}, u32[]{:S(2)}, u32[]{:S(2)}) collective-permute-start(bf16[1536,128]{1,0:T(8,128)(2,1)S(1)} %collective-permute-done.6.refs_4_), channel_id=1, source_target_pairs={{0,8},{4,12},{8,0},{12,4},{16,24},{20,28},{24,16},{28,20},{1,9},{5... | collective-permute-start | bytes 1179656 | tf_op jit(solution)/shard_map/ppermute | solution.py:398
  85.9 37.0 %all-to-all-start.2 = ((bf16[8,192,384]{2,1,0:T(8,128)(2,1)}), bf16[8,192,384]{2,1,0:T(8,128)(2,1)S(1)}, u32[]{:S(2)}, u32[]{:S(2)}) async-start(bf16[8,192,384]{2,1,0:T(8,128)(2,1)} %shard_map.72), calls=%async_computation.2 | async-start | bytes 2359296 | tf_op jit(solution)/shard_map/all_to_all | solution.py:691
  89.6 15.8 %collective-permute-start.7 = (bf16[8,240,128]{2,1,0:T(8,128)(2,1)S(1)}, bf16[8,240,128]{2,1,0:T(8,128)(2,1)S(1)}, u32[]{:S(2)}, u32[]{:S(2)}) collective-permute-start(bf16[8,240,128]{2,1,0:T(8,128)(2,1)S(1)} %slice.4.refs_0_), channel_id=1, source_target_pairs={{0,1},{1,0},{2,3},{3,2},{4,5},{5,4},{6,7},{7,6},{8,9},{9,8},{10,11... | collective-permute-start | bytes 1474568 | tf_op jit(solution)/shard_map/ppermute | solution.py:398
  89.7 15.7 %collective-permute-start.9 = (bf16[8,240,128]{2,1,0:T(8,128)(2,1)S(1)}, bf16[8,240,128]{2,1,0:T(8,128)(2,1)S(1)}, u32[]{:S(2)}, u32[]{:S(2)}) collective-permute-start(bf16[8,240,128]{2,1,0:T(8,128)(2,1)S(1)} %collective-permute-done.8.refs_2_), channel_id=1, source_target_pairs={{0,1},{1,0},{2,3},{3,2},{4,5},{5,4},{6,7},{7,6},{8,9},{9,8},{10,11... | collective-permute-start | bytes 1474568 | tf_op jit(solution)/shard_map/ppermute | solution.py:398
  90.2 23.3 %collective-permute-start.12 = (bf16[1536,128]{1,0:T(8,128)(2,1)S(1)}, bf16[1536,128]{1,0:T(8,128)(2,1)S(1)}, u32[]{:S(2)}, u32[]{:S(2)}) collective-permute-start(bf16[1536,128]{1,0:T(8,128)(2,1)S(1)} %collective-permute-done.6.refs_4_), channel_id=1, source_target_pairs={{0,4},{4,0},{8,12},{12,8},{16,20},{20,16},{24,28},{28,24},{1,5},{5... | collective-permute-start | bytes 1179656 | tf_op jit(solution)/shard_map/ppermute | solution.py:398
  105.4 14.9 %collective-permute-start.11 = (bf16[1536,128]{1,0:T(8,128)(2,1)}, bf16[1536,128]{1,0:T(8,128)(2,1)S(1)}, u32[]{:S(2)}, u32[]{:S(2)}) collective-permute-start(bf16[1536,128]{1,0:T(8,128)(2,1)} %collective-permute-done.10.refs_0_), channel_id=1, source_target_pairs={{0,4},{4,0},{8,12},{12,8},{16,20},{20,16},{24,28},{28,24},{1,5},{5... | collective-permute-start | bytes 1179656 | tf_op jit(solution)/shard_map/ppermute | solution.py:398
where the time goes:
time: 126 us; the launch traced here: 125 us
  waiting for transfers between devices  59.5 us (47%)
  Pallas kernels  30.8 us (24%)
  starting transfers between devices  28.3 us (22%)
  local copies, waits for them, and re-layouts  5.67 us (4%)
    ppermute x13, waiting for transfers between devices, exchange(): lax.ppermute(block, axis, [(i, i ^ bit) for i in range(lax.axis_size(axis...  54.4 us
    all_to_all x3, starting transfers between devices, swap(): lax.all_to_all(blocks, 'seq', split_axis=0, concat_axis=0, tiled=True)  15.4 us
    ppermute x13, starting transfers between devices, exchange(): lax.ppermute(block, axis, [(i, i ^ bit) for i in range(lax.axis_size(axis...  13 us
    pallas_call x1, Pallas kernels, backward(): pl.pallas_call(backward_kernel, in_specs=[SMEM_SPEC] + [pl.BlockSpec()] *...  7.53 us
    pallas_call x2, Pallas kernels, weight_part(): pl.pallas_call(functools.partial(weight_part_kernel, first, count), in_sp...  6.56 us
    all_to_all x3, waiting for transfers between devices, swap(): lax.all_to_all(blocks, 'seq', split_axis=0, concat_axis=0, tiled=True)  5.09 us
    unnamed x12, local copies, waits for them, and re-layouts  4.61 us
    pallas_call x1, Pallas kernels, grad_swap(): pl.pallas_call(functools.partial(grad_swap_kernel, count), grid_spec=pltp...  4.4 us
  transfers between devices with their start and end apart: 16, of which 7 were waited for; matrix products, arithmetic and copies ran while one was open for 1% of the time, Pallas kernels for 20%

commit v1 on v0

--- a/solution.py
+++ b/solution.py
@@ -552,8 +552,8 @@
 
 def masked_scores(start, keys, key_ref, query, live_ref):
     scores = dot_cols(key_ref[:keys], query) * (1.0 / math.sqrt(DH)) + live_ref[:keys, :1]
-    row = start + lax.broadcasted_iota(jnp.int32, (1, WIDE_BLOCK), 1)
-    key_pos = start + lax.broadcasted_iota(jnp.int32, (WIDE_BLOCK, 1), 0)
+    row = start + lax.broadcasted_iota(jnp.int32, (1, keys - start), 1)
+    key_pos = start + lax.broadcasted_iota(jnp.int32, (keys - start, 1), 0)
     edge = jnp.where(key_pos <= row, scores[start:], -1e30)
     return jnp.concatenate([scores[:start], edge], axis=0) if start else edge
 
@@ -630,9 +630,9 @@
     for shard in range(seq_count):
         grad_ref[shard * slots : (shard + 1) * slots] = grads_ref[shard, :slots]
     key_flip = key_ref[...].T
-    for start in range(0, query_ref.shape[0], WIDE_BLOCK):
-        rows = slice(start, start + WIDE_BLOCK)
-        keys = start + WIDE_BLOCK
+    for start in range(0, query_ref.shape[0], QUERY_BLOCK):
+        rows = slice(start, start + QUERY_BLOCK)
+        keys = start + QUERY_BLOCK
         query = query_ref[rows]
         grad = grad_ref[rows]
         scores = masked_scores(start, keys, key_ref, query, live_ref)

time: 126 us -> 125 us (level)
  transfers between devices with their start and end apart: 16 -> 16, of which waited for: 7 -> 7; matrix products, arithmetic and copies ran while one was open for 1% -> 1% of each run, Pallas kernels for 20% -> 19%
where the time goes in v1:
time: 125 us
  waiting for transfers between devices  59.5 us (48%)
  Pallas kernels  30.2 us (24%)
  starting transfers between devices  28.3 us (23%)
  local copies, waits for them, and re-layouts  5.67 us (5%)
    ppermute x13, waiting for transfers between devices, exchange(): lax.ppermute(block, axis, [(i, i ^ bit) for i in range(lax.axis_size(axis...  54.4 us
    all_to_all x3, starting transfers between devices, swap(): lax.all_to_all(blocks, 'seq', split_axis=0, concat_axis=0, tiled=True)  15.4 us
    ppermute x13, starting transfers between devices, exchange(): lax.ppermute(block, axis, [(i, i ^ bit) for i in range(lax.axis_size(axis...  13 us
    pallas_call x1, Pallas kernels, backward(): pl.pallas_call(backward_kernel, in_specs=[SMEM_SPEC] + [pl.BlockSpec()] *...  7 us
    pallas_call x2, Pallas kernels, weight_part(): pl.pallas_call(functools.partial(weight_part_kernel, first, count), in_sp...  6.56 us
    all_to_all x3, waiting for transfers between devices, swap(): lax.all_to_all(blocks, 'seq', split_axis=0, concat_axis=0, tiled=True)  5.09 us
    unnamed x12, local copies, waits for them, and re-layouts  4.61 us
    pallas_call x1, Pallas kernels, grad_swap(): pl.pallas_call(functools.partial(grad_swap_kernel, count), grid_spec=pltp...  4.4 us
  transfers between devices with their start and end apart: 16, of which 7 were waited for; matrix products, arithmetic and copies ran while one was open for 1% of the time, Pallas kernels for 19%

profile of v1, /device:TPU:0, one launch (start us, length us, event | category | flops | bytes accessed | tf_op | source)
XLA Modules:
  0.0 124.7 jit_solution(11772020313585789357)
XLA Ops:
  0.6 3.9 %shard_map.68 = bf16[8,192,384]{2,1,0:T(8,128)(2,1)} custom-call(s32[1,192]{1,0:T(1,128)} %index_ref.4, bf16[3,512,1024]{2,1,0:T(8,128)(2,1)} %bitcast.4), custom_call_target="tpu_custom_call" | custom-call | flops 603979776 | bytes 4194304 | tf_op jit(solution)/shard_map/pallas_call | solution.py:342
  4.5 7.4 %all-to-all-start = ((bf16[8,192,384]{2,1,0:T(8,128)(2,1)}), bf16[8,192,384]{2,1,0:T(8,128)(2,1)S(1)}, u32[]{:S(2)}, u32[]{:S(2)}) async-start(bf16[8,192,384]{2,1,0:T(8,128)(2,1)} %shard_map.68), calls=%async_computation | async-start | bytes 2359296 | tf_op jit(solution)/shard_map/all_to_all | solution.py:691
  12.4 1.6 %collective-permute-start.1 = (bf16[192,1280]{1,0:T(8,128)(2,1)S(1)}, bf16[192,1280]{1,0:T(8,128)(2,1)S(1)}, u32[]{:S(2)}, u32[]{:S(2)}) collective-permute-start(bf16[192,1280]{1,0:T(8,128)(2,1)S(1)} %shard_map.70.refs_0_), channel_id=1, source_target_pairs={{0,2},{1,3},{2,0},{3,1},{4,6},{5,7},{6,4},{7,5},{8,10},{9,11},{10,... | collective-permute-start | bytes 1474568 | tf_op jit(solution)/shard_map/ppermute | solution.py:398
  14.0 11.2 %collective-permute-done.1.refs_2_ = bf16[192,1280]{1,0:T(8,128)(2,1)S(1)} collective-permute-done((bf16[192,1280]{1,0:T(8,128)(2,1)S(1)}, bf16[192,1280]{1,0:T(8,128)(2,1)S(1)}, u32[]{:S(2)}, u32[]{:S(2)}) %collective-permute-start.1) | collective-permute-done | bytes 491552 | tf_op jit(solution)/shard_map/ppermute | solution.py:398
  25.2 1.8 %collective-permute-done.2.refs_3_ = bf16[192,1280]{1,0:T(8,128)(2,1)S(1)} collective-permute-done((bf16[192,1280]{1,0:T(8,128)(2,1)S(1)}, bf16[192,1280]{1,0:T(8,128)(2,1)S(1)}, u32[]{:S(2)}, u32[]{:S(2)}) %collective-permute-start.2) | collective-permute-done | bytes 491552 | tf_op jit(solution)/shard_map/ppermute | solution.py:398
  27.0 4.0 %copy-done = bf16[5120,1024]{1,0:T(8,128)(2,1)S(1)} copy-done((bf16[5120,1024]{1,0:T(8,128)(2,1)S(1)}, bf16[5120,1024]{1,0:T(8,128)(2,1)}, u32[]{:S(2)}) %copy-start) | copy-done | bytes 10485784
  31.0 4.4 %shard_map.71 = bf16[8,432,128]{2,1,0:T(8,128)(2,1)} custom-call(s32[2]{0:T(128)S(1)} %pad_add_fusion.place_ref, bf16[192,1280]{1,0:T(8,128)(2,1)S(1)} %shard_map.70.refs_0_, bf16[192,1280]{1,0:T(8,128)(2,1)S(1)} %collective-permute-done.refs_1_, bf16[192,1280]{1,0:T(8,128)(2,1)S(1)} %collective-permute-done.1.refs_2_, ...), custom_call_target="tpu_custom_call" | custom-call | flops 2013265920 | bytes 10485760 | tf_op jit(solution)/shard_map/pallas_call | solution.py:447
  35.4 5.1 %all-to-all-done.block_ref = bf16[8,192,384]{2,1,0:T(8,128)(2,1)S(1)} async-done(((bf16[8,192,384]{2,1,0:T(8,128)(2,1)}), bf16[8,192,384]{2,1,0:T(8,128)(2,1)S(1)}, u32[]{:S(2)}, u32[]{:S(2)}) %all-to-all-start) | async-done | bytes 1179680 | tf_op jit(solution)/shard_map/all_to_all | solution.py:691
  40.5 4.2 %all-to-all-start.1 = ((bf16[8,432,128]{2,1,0:T(8,128)(2,1)}), bf16[8,432,128]{2,1,0:T(8,128)(2,1)}, u32[]{:S(2)}, u32[]{:S(2)}) async-start(bf16[8,432,128]{2,1,0:T(8,128)(2,1)} %shard_map.71), calls=%async_computation.1 | async-start | bytes 1769472 | tf_op jit(solution)/shard_map/all_to_all | solution.py:691
  44.7 4.3 %shard_map.69 = (bf16[1536,128]{1,0:T(8,128)(2,1)}, f32[8,1536]{1,0:T(8,128)S(1)}) custom-call(s32[8]{0:T(128)S(1)} %copy-done.4, bf16[8,192,384]{2,1,0:T(8,128)(2,1)S(1)} %all-to-all-done.block_ref), custom_call_target="tpu_custom_call" | custom-call | flops 603979776 | bytes 3145728 | tf_op jit(solution)/shard_map/pallas_call | solution.py:597
  49.7 1.9 %collective-permute-start.4 = (bf16[1536,128]{1,0:T(8,128)(2,1)}, bf16[1536,128]{1,0:T(8,128)(2,1)S(1)}, u32[]{:S(2)}, u32[]{:S(2)}) collective-permute-start(bf16[1536,128]{1,0:T(8,128)(2,1)} %get-tuple-element.12.attended_ref.refs_0_), channel_id=1, source_target_pairs={{0,8},{4,12},{8,0},{12,4},{16,24},{20,28},{24,16},{28,20},{1,9},{5... | collective-permute-start | bytes 1179656 | tf_op jit(solution)/shard_map/ppermute | solution.py:398
  51.5 2.4 %collective-permute-start.6 = (bf16[1536,128]{1,0:T(8,128)(2,1)}, bf16[1536,128]{1,0:T(8,128)(2,1)S(1)}, u32[]{:S(2)}, u32[]{:S(2)}) collective-permute-start(bf16[1536,128]{1,0:T(8,128)(2,1)} %get-tuple-element.12.attended_ref.refs_0_), channel_id=1, source_target_pairs={{0,16},{4,20},{8,24},{12,28},{16,0},{20,4},{24,8},{28,12},{1,17},{... | collective-permute-start | bytes 1179656 | tf_op jit(solution)/shard_map/ppermute | solution.py:398
  55.4 18.4 %collective-permute-done.4.refs_2_ = bf16[1536,128]{1,0:T(8,128)(2,1)S(1)} collective-permute-done((bf16[1536,128]{1,0:T(8,128)(2,1)}, bf16[1536,128]{1,0:T(8,128)(2,1)S(1)}, u32[]{:S(2)}, u32[]{:S(2)}) %collective-permute-start.4) | collective-permute-done | bytes 393248 | tf_op jit(solution)/shard_map/ppermute | solution.py:398
  73.9 1.7 %collective-permute-start.5 = (bf16[1536,128]{1,0:T(8,128)(2,1)S(1)}, bf16[1536,128]{1,0:T(8,128)(2,1)}, u32[]{:S(2)}, u32[]{:S(2)}) collective-permute-start(bf16[1536,128]{1,0:T(8,128)(2,1)S(1)} %collective-permute-done.4.refs_2_), channel_id=1, source_target_pairs={{0,4},{4,0},{8,12},{12,8},{16,20},{20,16},{24,28},{28,24},{1,5},{5... | collective-permute-start | bytes 1179656 | tf_op jit(solution)/shard_map/ppermute | solution.py:398
  76.7 1.6 %collective-permute-start.8 = (bf16[8,240,128]{2,1,0:T(8,128)(2,1)S(1)}, bf16[8,240,128]{2,1,0:T(8,128)(2,1)S(1)}, u32[]{:S(2)}, u32[]{:S(2)}) collective-permute-start(bf16[8,240,128]{2,1,0:T(8,128)(2,1)S(1)} %slice.4.refs_0_), channel_id=1, source_target_pairs={{0,2},{1,3},{2,0},{3,1},{4,6},{5,7},{6,4},{7,5},{8,10},{9,11},{10,... | collective-permute-start | bytes 1474568 | tf_op jit(solution)/shard_map/ppermute | solution.py:398
  78.2 7.0 %shard_map.72 = bf16[8,192,384]{2,1,0:T(8,128)(2,1)} custom-call(s32[8]{0:T(128)} %count_ref.3, bf16[8,192,384]{2,1,0:T(8,128)(2,1)} %copy-done.2, bf16[1536,128]{1,0:T(8,128)(2,1)} %get-tuple-element.12.attended_ref.refs_0_, f32[8,1536]{1,0:T(8,128)} %copy-done.5, bf16[8,432,128]{2,1,0:T(8,128)(2,1)} %all-to-all-done.1.grads_ref), custom_call_target="tpu_custom_call" | custom-call | flops 1509949440 | bytes 3145728 | tf_op jit(solution)/shard_map/pallas_call | solution.py:662
  85.3 3.8 %all-to-all-start.2 = ((bf16[8,192,384]{2,1,0:T(8,128)(2,1)}), bf16[8,192,384]{2,1,0:T(8,128)(2,1)S(1)}, u32[]{:S(2)}, u32[]{:S(2)}) async-start(bf16[8,192,384]{2,1,0:T(8,128)(2,1)} %shard_map.72), calls=%async_computation.2 | async-start | bytes 2359296 | tf_op jit(solution)/shard_map/all_to_all | solution.py:691
  89.7 1.7 %collective-permute-start.12 = (bf16[1536,128]{1,0:T(8,128)(2,1)S(1)}, bf16[1536,128]{1,0:T(8,128)(2,1)S(1)}, u32[]{:S(2)}, u32[]{:S(2)}) collective-permute-start(bf16[1536,128]{1,0:T(8,128)(2,1)S(1)} %collective-permute-done.6.refs_4_), channel_id=1, source_target_pairs={{0,4},{4,0},{8,12},{12,8},{16,20},{20,16},{24,28},{28,24},{1,5},{5... | collective-permute-start | bytes 1179656 | tf_op jit(solution)/shard_map/ppermute | solution.py:398
  91.4 13.5 %collective-permute-done.10.refs_0_ = bf16[1536,128]{1,0:T(8,128)(2,1)} collective-permute-done((bf16[1536,128]{1,0:T(8,128)(2,1)S(1)}, bf16[1536,128]{1,0:T(8,128)(2,1)}, u32[]{:S(2)}, u32[]{:S(2)}) %collective-permute-start.10) | collective-permute-done | bytes 393248 | tf_op jit(solution)/shard_map/ppermute | solution.py:398
  106.4 6.6 %collective-permute-done.12.refs_5_ = bf16[1536,128]{1,0:T(8,128)(2,1)S(1)} collective-permute-done((bf16[1536,128]{1,0:T(8,128)(2,1)S(1)}, bf16[1536,128]{1,0:T(8,128)(2,1)S(1)}, u32[]{:S(2)}, u32[]{:S(2)}) %collective-permute-start.12) | collective-permute-done | bytes 393248 | tf_op jit(solution)/shard_map/ppermute | solution.py:398
  113.0 4.0 %shard_map.75.refs_2_ = f32[640,1024]{1,0:T(8,128)} custom-call(s32[2]{0:T(128)S(1)} %pad_add_fusion.place_ref, bf16[640,1536]{1,0:T(8,128)(2,1)S(1)} %shard_map.74.flip_ref, bf16[1536,128]{1,0:T(8,128)(2,1)} %get-tuple-element.12.attended_ref.refs_0_, bf16[1536,128]{1,0:T(8,128)(2,1)} %collective-permute-done.3.refs_1_, ...), custom_call_target="tpu_custom_call" | custom-call | flops 1509949440 | bytes 9437184 | tf_op jit(solution)/shard_map/pallas_call | solution.py:524
  117.0 2.8 %collective-permute-done.11.refs_1_ = bf16[1536,128]{1,0:T(8,128)(2,1)S(1)} collective-permute-done((bf16[1536,128]{1,0:T(8,128)(2,1)}, bf16[1536,128]{1,0:T(8,128)(2,1)S(1)}, u32[]{:S(2)}, u32[]{:S(2)}) %collective-permute-start.11) | collective-permute-done | bytes 393248 | tf_op jit(solution)/shard_map/ppermute | solution.py:398
  119.8 2.5 %shard_map.76 = f32[640,1024]{1,0:T(8,128)} custom-call(s32[2]{0:T(128)S(1)} %pad_add_fusion.place_ref, bf16[640,1536]{1,0:T(8,128)(2,1)S(1)} %shard_map.74.flip_ref, bf16[1536,128]{1,0:T(8,128)(2,1)} %collective-permute-done.10.refs_0_, bf16[1536,128]{1,0:T(8,128)(2,1)S(1)} %collective-permute-done.11.refs_1_, ...), custom_call_target="tpu_custom_call", output_to_operand_aliasing={{}: (4, {})} | custom-call | flops 14092861440 | bytes 3145728 | tf_op jit(solution)/shard_map/pallas_call | solution.py:524
  122.4 2.2 %shard_map.73 = bf16[3,512,1024]{2,1,0:T(8,128)(2,1)} custom-call(s32[1,192]{1,0:T(1,128)S(1)} %copy-done.3, bf16[8,192,384]{2,1,0:T(8,128)(2,1)S(1)} %all-to-all-done.2.rows_ref), custom_call_target="tpu_custom_call" | custom-call | tf_op jit(solution)/shard_map/pallas_call | solution.py:384
  (31 shorter events, 5.8 us)
Async XLA Ops:
  4.5 7.4 %copy-start.1 = (bf16[512,1280]{1,0:T(8,128)(2,1)S(1)}, bf16[512,1280]{1,0:T(8,128)(2,1)}, u32[]{:S(2)}) copy-start(bf16[512,1280]{1,0:T(8,128)(2,1)} %grad_ref.1) | copy-start | bytes 3932164
  4.5 7.4 %copy-start.3 = (s32[1,192]{1,0:T(1,128)S(1)}, s32[1,192]{1,0:T(1,128)}, u32[]{:S(2)}) copy-start(s32[1,192]{1,0:T(1,128)} %index_ref.4) | copy-start | bytes 2308
  4.5 36.0 %all-to-all-start = ((bf16[8,192,384]{2,1,0:T(8,128)(2,1)}), bf16[8,192,384]{2,1,0:T(8,128)(2,1)S(1)}, u32[]{:S(2)}, u32[]{:S(2)}) async-start(bf16[8,192,384]{2,1,0:T(8,128)(2,1)} %shard_map.68), calls=%async_computation | async-start | bytes 2359296 | tf_op jit(solution)/shard_map/all_to_all | solution.py:691
  12.4 12.7 %collective-permute-start.1 = (bf16[192,1280]{1,0:T(8,128)(2,1)S(1)}, bf16[192,1280]{1,0:T(8,128)(2,1)S(1)}, u32[]{:S(2)}, u32[]{:S(2)}) collective-permute-start(bf16[192,1280]{1,0:T(8,128)(2,1)S(1)} %shard_map.70.refs_0_), channel_id=1, source_target_pairs={{0,2},{1,3},{2,0},{3,1},{4,6},{5,7},{6,4},{7,5},{8,10},{9,11},{10,... | collective-permute-start | bytes 1474568 | tf_op jit(solution)/shard_map/ppermute | solution.py:398
  14.0 11.2 %collective-permute-start = (bf16[192,1280]{1,0:T(8,128)(2,1)S(1)}, bf16[192,1280]{1,0:T(8,128)(2,1)S(1)}, u32[]{:S(2)}, u32[]{:S(2)}) collective-permute-start(bf16[192,1280]{1,0:T(8,128)(2,1)S(1)} %shard_map.70.refs_0_), channel_id=1, source_target_pairs={{0,1},{1,0},{2,3},{3,2},{4,5},{5,4},{6,7},{7,6},{8,9},{9,8},{10,11... | collective-permute-start | bytes 1474568 | tf_op jit(solution)/shard_map/ppermute | solution.py:398
  25.1 1.9 %collective-permute-start.2 = (bf16[192,1280]{1,0:T(8,128)(2,1)S(1)}, bf16[192,1280]{1,0:T(8,128)(2,1)S(1)}, u32[]{:S(2)}, u32[]{:S(2)}) collective-permute-start(bf16[192,1280]{1,0:T(8,128)(2,1)S(1)} %collective-permute-done.1.refs_2_), channel_id=1, source_target_pairs={{0,1},{1,0},{2,3},{3,2},{4,5},{5,4},{6,7},{7,6},{8,9},{9,8},{10,11... | collective-permute-start | bytes 1474568 | tf_op jit(solution)/shard_map/ppermute | solution.py:398
  25.1 19.6 %copy-start.4 = (s32[8]{0:T(128)S(1)}, s32[8]{0:T(128)}, u32[]{:S(2)}) copy-start(s32[8]{0:T(128)} %count_ref.3) | copy-start | bytes 100
  27.0 4.0 %copy-start = (bf16[5120,1024]{1,0:T(8,128)(2,1)S(1)}, bf16[5120,1024]{1,0:T(8,128)(2,1)}, u32[]{:S(2)}) copy-start(bf16[5120,1024]{1,0:T(8,128)(2,1)} %refs_4_.1) | copy-start | bytes 31457284
  40.5 8.6 %copy-start.2 = (bf16[8,192,384]{2,1,0:T(8,128)(2,1)}, bf16[8,192,384]{2,1,0:T(8,128)(2,1)S(1)}, u32[]{:S(2)}) copy-start(bf16[8,192,384]{2,1,0:T(8,128)(2,1)S(1)} %all-to-all-done.block_ref) | copy-start | bytes 3538948
  40.5 35.1 %all-to-all-start.1 = ((bf16[8,432,128]{2,1,0:T(8,128)(2,1)}), bf16[8,432,128]{2,1,0:T(8,128)(2,1)}, u32[]{:S(2)}, u32[]{:S(2)}) async-start(bf16[8,432,128]{2,1,0:T(8,128)(2,1)} %shard_map.71), calls=%async_computation.1 | async-start | bytes 1769472 | tf_op jit(solution)/shard_map/all_to_all | solution.py:691
  49.0 0.6 copy-start.5
  49.7 24.2 %collective-permute-start.4 = (bf16[1536,128]{1,0:T(8,128)(2,1)}, bf16[1536,128]{1,0:T(8,128)(2,1)S(1)}, u32[]{:S(2)}, u32[]{:S(2)}) collective-permute-start(bf16[1536,128]{1,0:T(8,128)(2,1)} %get-tuple-element.12.attended_ref.refs_0_), channel_id=1, source_target_pairs={{0,8},{4,12},{8,0},{12,4},{16,24},{20,28},{24,16},{28,20},{1,9},{5... | collective-permute-start | bytes 1179656 | tf_op jit(solution)/shard_map/ppermute | solution.py:398
  51.5 33.7 %collective-permute-start.6 = (bf16[1536,128]{1,0:T(8,128)(2,1)}, bf16[1536,128]{1,0:T(8,128)(2,1)S(1)}, u32[]{:S(2)}, u32[]{:S(2)}) collective-permute-start(bf16[1536,128]{1,0:T(8,128)(2,1)} %get-tuple-element.12.attended_ref.refs_0_), channel_id=1, source_target_pairs={{0,16},{4,20},{8,24},{12,28},{16,0},{20,4},{24,8},{28,12},{1,17},{... | collective-permute-start | bytes 1179656 | tf_op jit(solution)/shard_map/ppermute | solution.py:398
  53.9 31.3 %collective-permute-start.3 = (bf16[1536,128]{1,0:T(8,128)(2,1)}, bf16[1536,128]{1,0:T(8,128)(2,1)}, u32[]{:S(2)}, u32[]{:S(2)}) collective-permute-start(bf16[1536,128]{1,0:T(8,128)(2,1)} %get-tuple-element.12.attended_ref.refs_0_), channel_id=1, source_target_pairs={{0,4},{4,0},{8,12},{12,8},{16,20},{20,16},{24,28},{28,24},{1,5},{5... | collective-permute-start | bytes 1179656 | tf_op jit(solution)/shard_map/ppermute | solution.py:398
  73.9 11.4 %collective-permute-start.5 = (bf16[1536,128]{1,0:T(8,128)(2,1)S(1)}, bf16[1536,128]{1,0:T(8,128)(2,1)}, u32[]{:S(2)}, u32[]{:S(2)}) collective-permute-start(bf16[1536,128]{1,0:T(8,128)(2,1)S(1)} %collective-permute-done.4.refs_2_), channel_id=1, source_target_pairs={{0,4},{4,0},{8,12},{12,8},{16,20},{20,16},{24,28},{28,24},{1,5},{5... | collective-permute-start | bytes 1179656 | tf_op jit(solution)/shard_map/ppermute | solution.py:398
  76.7 12.5 %collective-permute-start.8 = (bf16[8,240,128]{2,1,0:T(8,128)(2,1)S(1)}, bf16[8,240,128]{2,1,0:T(8,128)(2,1)S(1)}, u32[]{:S(2)}, u32[]{:S(2)}) collective-permute-start(bf16[8,240,128]{2,1,0:T(8,128)(2,1)S(1)} %slice.4.refs_0_), channel_id=1, source_target_pairs={{0,2},{1,3},{2,0},{3,1},{4,6},{5,7},{6,4},{7,5},{8,10},{9,11},{10,... | collective-permute-start | bytes 1474568 | tf_op jit(solution)/shard_map/ppermute | solution.py:398
  85.3 19.6 %collective-permute-start.10 = (bf16[1536,128]{1,0:T(8,128)(2,1)S(1)}, bf16[1536,128]{1,0:T(8,128)(2,1)}, u32[]{:S(2)}, u32[]{:S(2)}) collective-permute-start(bf16[1536,128]{1,0:T(8,128)(2,1)S(1)} %collective-permute-done.6.refs_4_), channel_id=1, source_target_pairs={{0,8},{4,12},{8,0},{12,4},{16,24},{20,28},{24,16},{28,20},{1,9},{5... | collective-permute-start | bytes 1179656 | tf_op jit(solution)/shard_map/ppermute | solution.py:398
  85.3 37.0 %all-to-all-start.2 = ((bf16[8,192,384]{2,1,0:T(8,128)(2,1)}), bf16[8,192,384]{2,1,0:T(8,128)(2,1)S(1)}, u32[]{:S(2)}, u32[]{:S(2)}) async-start(bf16[8,192,384]{2,1,0:T(8,128)(2,1)} %shard_map.72), calls=%async_computation.2 | async-start | bytes 2359296 | tf_op jit(solution)/shard_map/all_to_all | solution.py:691
  89.1 15.8 %collective-permute-start.7 = (bf16[8,240,128]{2,1,0:T(8,128)(2,1)S(1)}, bf16[8,240,128]{2,1,0:T(8,128)(2,1)S(1)}, u32[]{:S(2)}, u32[]{:S(2)}) collective-permute-start(bf16[8,240,128]{2,1,0:T(8,128)(2,1)S(1)} %slice.4.refs_0_), channel_id=1, source_target_pairs={{0,1},{1,0},{2,3},{3,2},{4,5},{5,4},{6,7},{7,6},{8,9},{9,8},{10,11... | collective-permute-start | bytes 1474568 | tf_op jit(solution)/shard_map/ppermute | solution.py:398
  89.2 15.7 %collective-permute-start.9 = (bf16[8,240,128]{2,1,0:T(8,128)(2,1)S(1)}, bf16[8,240,128]{2,1,0:T(8,128)(2,1)S(1)}, u32[]{:S(2)}, u32[]{:S(2)}) collective-permute-start(bf16[8,240,128]{2,1,0:T(8,128)(2,1)S(1)} %collective-permute-done.8.refs_2_), channel_id=1, source_target_pairs={{0,1},{1,0},{2,3},{3,2},{4,5},{5,4},{6,7},{7,6},{8,9},{9,8},{10,11... | collective-permute-start | bytes 1474568 | tf_op jit(solution)/shard_map/ppermute | solution.py:398
  89.7 23.3 %collective-permute-start.12 = (bf16[1536,128]{1,0:T(8,128)(2,1)S(1)}, bf16[1536,128]{1,0:T(8,128)(2,1)S(1)}, u32[]{:S(2)}, u32[]{:S(2)}) collective-permute-start(bf16[1536,128]{1,0:T(8,128)(2,1)S(1)} %collective-permute-done.6.refs_4_), channel_id=1, source_target_pairs={{0,4},{4,0},{8,12},{12,8},{16,20},{20,16},{24,28},{28,24},{1,5},{5... | collective-permute-start | bytes 1179656 | tf_op jit(solution)/shard_map/ppermute | solution.py:398
  104.9 14.9 %collective-permute-start.11 = (bf16[1536,128]{1,0:T(8,128)(2,1)}, bf16[1536,128]{1,0:T(8,128)(2,1)S(1)}, u32[]{:S(2)}, u32[]{:S(2)}) collective-permute-start(bf16[1536,128]{1,0:T(8,128)(2,1)} %collective-permute-done.10.refs_0_), channel_id=1, source_target_pairs={{0,4},{4,0},{8,12},{12,8},{16,20},{20,16},{24,28},{28,24},{1,5},{5... | collective-permute-start | bytes 1179656 | tf_op jit(solution)/shard_map/ppermute | solution.py:398
